TPU v7x, 32 devices: a whole 2x2x4 slice. The times are simulated.
32 devices in a mesh: pairs: 4 (over y, x), rows: 2 (over core), cols: 4 (over z).
Axes of the slice: x: 2, y: 2, z: 4, core: 2. Of those that a mesh axis runs over, the one named last changes fastest.
Arguments:
- frame_one: bfloat16 [4, 1536, 128], P('pairs', 'rows'), may hold values from -16 to 16
- frame_two: bfloat16 [4, 1536, 128], P('pairs', ('rows', 'cols')), may hold values from -16 to 16
- weight: bfloat16 [128, 128], replicated, may hold values from -0.5 to 0.5
- flow_cot: float32 [4, 2, 1536], P('pairs', None, 'rows'), may hold values from -60 to 60
Outputs:
- flow: float32 [4, 2, 1536], P('pairs', None, 'rows')
- grad_one: float32 [4, 1536, 128], P('pairs', 'rows')
- grad_two: float32 [4, 1536, 128], P('pairs', ('rows', 'cols'))
- grad_w: float32 [128, 128], replicated
All inputs are finite; a program needn't handle non-finite values.
Results may differ from a plain program's by a relative error of at most 0.002.
The roundings to bfloat16 on the way count: a program that leaves them out, or rounds other values in their place, can miss the bound.
Values may be sent and summed in bfloat16 or wider, within the bound.
A program may use at most 64 MiB of HBM per device.

v0:
```python
import math

import jax
import jax.numpy as jnp
from jax import lax
from jax.sharding import PartitionSpec as P

IMG_W = 128


coord_unit = 0.0625


def coords(index):
    return (
        jnp.stack([(index % IMG_W).astype(jnp.float32), (index // IMG_W).astype(jnp.float32)])
        * coord_unit
    )


def slopes(feat_q, feat_k, coord_k, top, total, cot_x, cot_y, offset, scale):
    scores = jnp.dot(feat_q, feat_k.T, preferred_element_type=jnp.float32) * scale
    prob = jnp.exp(scores - top[:, None]) / total[:, None]
    inner = cot_x[:, None] * coord_k[0][None, :] + cot_y[:, None] * coord_k[1][None, :]
    return (prob * (inner - offset[:, None])).astype(jnp.bfloat16)


def lead_product(left, right, highest):
    if highest:
        return lax.dot_general(
            left,
            right,
            (((0,), (0,)), ((), ())),
            precision=lax.Precision.HIGHEST,
            preferred_element_type=jnp.float32,
        )
    return lax.dot_general(
        left, right, (((0,), (0,)), ((), ())), preferred_element_type=jnp.float32
    )


def shards(frame_one, frame_two, weight, flow_cot):
    chan = weight.shape[0]
    scale = 1.0 / math.sqrt(chan)
    qrows = frame_one.shape[1]
    krows = frame_two.shape[1]
    nrows = lax.axis_size("rows")
    ncols = lax.axis_size("cols")
    row_id = lax.axis_index("rows")
    col_id = lax.axis_index("cols")
    x_one = frame_one[0]
    x_two = frame_two[0]
    cot = flow_cot[0]
    feat_one = jnp.dot(x_one, weight, preferred_element_type=jnp.float32).astype(jnp.bfloat16)
    feat_two = jnp.dot(x_two, weight, preferred_element_type=jnp.float32).astype(jnp.bfloat16)
    query_coords = coords(row_id * qrows + jnp.arange(qrows, dtype=jnp.int32))
    gathered = lax.all_gather(feat_two, "rows", axis=0, tiled=True)
    kcol = gathered.shape[0]
    width = min(512, kcol)
    nblk = kcol // width
    local = jnp.arange(kcol, dtype=jnp.int32)
    key_index = (local // krows * ncols + col_id) * krows + local % krows
    key_coords = coords(key_index)
    key_blocks = gathered.reshape(nblk, width, chan)
    coord_blocks = key_coords.reshape(2, nblk, width).transpose(1, 0, 2)

    def forward(carry, blk):
        top, total, sum_x, sum_y = carry
        block_keys, block_coords = blk
        scores = jnp.dot(feat_one, block_keys.T, preferred_element_type=jnp.float32) * scale
        new_top = jnp.maximum(top, jnp.max(scores, axis=1))
        shrink = jnp.exp(top - new_top)
        expo = jnp.exp(scores - new_top[:, None])
        total = total * shrink + jnp.sum(expo, axis=1)
        sum_x = sum_x * shrink + jnp.dot(expo, block_coords[0], precision=lax.Precision.HIGHEST)
        sum_y = sum_y * shrink + jnp.dot(expo, block_coords[1], precision=lax.Precision.HIGHEST)
        return ((new_top, total, sum_x, sum_y), None)

    zeros_q = jnp.zeros((qrows,), jnp.float32)
    start_carry = (jnp.full((qrows,), -1e30, jnp.float32), zeros_q, zeros_q, zeros_q)
    (top, total, sum_x, sum_y), _ = lax.scan(forward, start_carry, (key_blocks, coord_blocks))
    peak = lax.pmax(top, "cols")
    shrink = jnp.exp(top - peak)
    total, sum_x, sum_y = lax.psum((total * shrink, sum_x * shrink, sum_y * shrink), "cols")
    top = peak
    mean_x = sum_x / total
    mean_y = sum_y / total
    flow = jnp.stack([mean_x, mean_y]) - query_coords
    cot_x = cot[0]
    cot_y = cot[1]
    offset = cot_x * mean_x + cot_y * mean_y

    def backward(acc, blk):
        block_keys, block_coords = blk
        slope = slopes(feat_one, block_keys, block_coords, top, total, cot_x, cot_y, offset, scale)
        acc = acc + jnp.dot(slope, block_keys, preferred_element_type=jnp.float32) * scale
        return (acc, lead_product(slope, feat_one, False) * scale)

    part_one, terms = lax.scan(
        backward, jnp.zeros((qrows, chan), jnp.float32), (key_blocks, coord_blocks)
    )
    feat_two_grad = lax.psum_scatter(
        terms.reshape(kcol, chan), "rows", scatter_dimension=0, tiled=True
    )
    feat_one_grad = lax.psum(part_one, "cols")
    contract = (((1,), (1,)), ((), ()))
    grad_one = lax.dot_general(
        feat_one_grad.astype(jnp.bfloat16), weight, contract, preferred_element_type=jnp.float32
    )
    grad_two = lax.dot_general(
        feat_two_grad.astype(jnp.bfloat16), weight, contract, preferred_element_type=jnp.float32
    )
    term = lead_product(x_one.astype(jnp.float32), part_one, True) + lead_product(
        x_two.astype(jnp.float32), feat_two_grad, True
    )
    npairs = lax.axis_size("pairs") * frame_one.shape[0]
    grad_w = lax.psum(term, ("pairs", "rows", "cols")) / math.sqrt(npairs * qrows * nrows)
    return (flow[None], grad_one[None], grad_two[None], grad_w)


def solution(mesh):
    in_specs = (
        P("pairs", "rows", None),
        P("pairs", ("rows", "cols"), None),
        P(),
        P("pairs", None, "rows"),
    )
    out_specs = (
        P("pairs", None, "rows"),
        P("pairs", "rows", None),
        P("pairs", ("rows", "cols"), None),
        P(),
    )
    return jax.shard_map(shards, mesh=mesh, in_specs=in_specs, out_specs=out_specs, check_vma=False)
```

profile of v0, /device:TPU:0, one launch (start us, length us, event | category | flops | bytes accessed | tf_op | source)
XLA Modules:
  0.0 197.2 jit_solution(12528391213439726551)
XLA Ops:
  7.2 0.0 copy-start
  7.2 0.0 reduce-scatter.2.cloned.1.call-start
  7.2 0.9 copy-done
  8.1 0.9 convolution_convert_fusion
  9.0 0.9 convolution_convert_fusion.1
  10.0 2.0 %all_gather.3 = bf16[384,128]{1,0:T(8,128)(2,1)S(1)} all-gather(bf16[192,128]{1,0:T(8,128)(2,1)S(1)} %convolution_convert_fusion.1), channel_id=1, replica_groups=mesh['pairs'=4,'rows'=2,'cols'=4] {'rows'}, dimensions={0}, use_global_device_ids=true | all-gather | bytes 147456 | tf_op jit(solution)/shard_map/all_gather | solution.py:57
  12.0 0.3 fusion.23
  12.4 13.3 %pmax.7 = f32[768]{0:T(1024)S(1)} all-reduce(f32[768]{0:T(1024)S(1)} %broadcast_maximum_fusion), channel_id=1, replica_groups=mesh['pairs'=4,'rows'=2,'cols'=4] {'cols'}, use_global_device_ids=true, to_apply=%region_1.2 | all-reduce | flops 768 | bytes 6144 | tf_op jit(solution)/shard_map/pmax | solution.py:82
  25.7 0.8 convolution_reduce_fusion.1
  26.5 0.0 copy-start.3
  26.5 0.8 convolution_reduce_fusion
  27.4 0.2 fusion.1
  27.6 0.0 copy-done.3
  27.7 15.5 %all-reduce = (f32[768]{0:T(1024)S(1)}, f32[768]{0:T(1024)S(1)}, f32[768]{0:T(1024)S(1)}) all-reduce(f32[768]{0:T(1024)S(1)} %get-tuple-element.76, f32[768]{0:T(1024)S(1)} %get-tuple-element.77, f32[768]{0:T(1024)S(1)} %get-tuple-element.64), channel_id=1, replica_groups=mesh['pairs'=4,'rows'=2,'cols'=4] {'cols'}, use_global_device_ids=true, to_apply=%region_5.6 | all-reduce | flops 2304 | bytes 18432 | tf_op jit(solution)/shard_map/psum | solution.py:84
  43.2 0.4 multiply_convert_fusion
  43.6 1.0 convolution_multiply_fusion.2
  44.6 0.0 reduce-scatter.2.cloned.1.call-update
  44.6 0.0 copy-start.1
  44.6 0.0 all-reduce.4.cloned.1.call-start
  44.7 0.4 convolution_multiply_fusion.1
  45.1 0.0 copy-start.2
  45.1 0.5 fusion.4
  45.6 0.6 maximum_subtract_fusion
  46.2 22.8 %all-reduce.5 = bf16[768,128]{1,0:T(8,128)(2,1)S(1)} all-reduce(f32[768,128]{1,0:T(8,128)S(1)} %convolution_multiply_fusion.1), channel_id=1, replica_groups=mesh['pairs'=4,'rows'=2,'cols'=4] {'cols'}, use_global_device_ids=true, to_apply=%region_6.7 | all-reduce | flops 98304 | bytes 589824 | tf_op jit(solution)/shard_map/psum | solution.py:105
  69.0 0.0 copy-done.1
  69.0 1.0 convolution_bitcast_fusion
  70.0 0.0 reduce-scatter.2.cloned.1.call-done
  70.0 0.0 copy-done.2
  70.0 1.8 fusion
  71.8 0.0 all-reduce.4.cloned.1.call-update
  71.9 1.7 convolution_bitcast_fusion.1
  73.5 115.3 %all-reduce.4.cloned.1.call-done = f32[128,128]{0,1:T(8,128)} async-done(((f32[128,128]{0,1:T(8,128)}), f32[128,128]{0,1:T(8,128)}) %all-reduce.4.cloned.1.call-update) | async-done | bytes 65552 | tf_op jit(solution)/shard_map/psum | solution.py:117
  188.8 0.8 broadcast_multiply_fusion
  189.7 0.7 copy.8
  (10 shorter events, 0.1 us)
Async XLA Ops:
  7.2 0.9 copy-start
  7.2 62.8 %reduce-scatter.2.cloned.1.call-start = ((), (), s32[]{:S(2)}) async-start(), calls=%async_computation.1 | async-start | bytes 294912 | tf_op jit(solution)/shard_map/reduce_scatter | solution.py:102
  26.5 1.1 copy-start.3
  44.6 24.4 %copy-start.1 = (bf16[128,128]{1,0:T(8,128)(2,1)S(1)}, bf16[128,128]{1,0:T(8,128)(2,1)}, u32[]{:S(2)}) copy-start(bf16[128,128]{1,0:T(8,128)(2,1)} %param.6) | copy-start | bytes 98308
  44.6 144.2 %all-reduce.4.cloned.1.call-start = ((), (), s32[]{:S(2)}) async-start(), calls=%async_computation.2 | async-start | bytes 131072 | tf_op jit(solution)/shard_map/psum | solution.py:117
  45.1 24.9 %copy-start.2 = (bf16[1,192,128]{2,1,0:T(8,128)(2,1)S(1)}, bf16[1,192,128]{2,1,0:T(8,128)(2,1)}, u32[]{:S(2)}) copy-start(bf16[1,192,128]{2,1,0:T(8,128)(2,1)} %param.5) | copy-start | bytes 147460
Sparse Core Ops, SparseCore 0:
  44.7 6.0 reduce-scatter.1
  72.0 116.8 all-reduce.3
where the time goes:
time: 199 us; the launch traced here: 197 us
  waiting for transfers between devices  115 us (58%)
  blocking collectives  53.6 us (27%)
  between operations  14.2 us (7%)
  matrix products  10.2 us (5%)
  other arithmetic  2.13 us (1%)
    psum x1, waiting for transfers between devices, shards(): lax.psum(term, ('pairs', 'rows', 'cols'))  115 us
    psum x1, blocking collectives, shards(): feat_one_grad = lax.psum(part_one, 'cols')  22.8 us
    psum x1, blocking collectives, shards(): lax.psum((total * shrink, sum_x * shrink, sum_y * shrink), 'cols')  15.5 us
    pmax x1, blocking collectives, shards(): peak = lax.pmax(top, 'cols')  13.3 us
  transfers between devices with their start and end apart: 2, of which 1 were waited for; matrix products, arithmetic and copies ran while one was open for 2% of the time, Pallas kernels for 0%

commit v1 on v0

--- a/solution.py
+++ b/solution.py
@@ -1,11 +1,15 @@
+import functools
 import math
 
 import jax
 import jax.numpy as jnp
 from jax import lax
+from jax.experimental import pallas as pl
+from jax.experimental.pallas import tpu as pltpu
 from jax.sharding import PartitionSpec as P
 
 IMG_W = 128
+MESH = pl.DeviceIdType.MESH
 
 
 coord_unit = 0.0625
@@ -118,6 +122,278 @@
     return (flow[None], grad_one[None], grad_two[None], grad_w)
 
 
+def pieces(value):
+    high = value.astype(jnp.bfloat16)
+    rest = value - high.astype(jnp.float32)
+    mid = rest.astype(jnp.bfloat16)
+    low = (rest - mid.astype(jnp.float32)).astype(jnp.bfloat16)
+    return high, mid, low
+
+
+def last_dims(left, right):
+    return lax.dot_general(
+        left, right, (((1,), (1,)), ((), ())), preferred_element_type=jnp.float32
+    )
+
+
+def fused(
+    npairs, ncols,
+    x1_ref, x2_ref, w_ref, cot_ref,
+    flow_ref, g1_ref, g2_ref, gw_ref,
+    x2all, p1s, score, slope, left, table, two_out, two_in, terms, blocks,
+    z_send, z_recv, s_send, s_recv, t_send, t_recv, b_send, b_recv,
+):
+    qrows, chan = x1_ref.shape[1:]
+    krows = x2_ref.shape[1]
+    keys = x2all.shape[0]
+    chip = 2 * krows
+    part = chan // ncols
+    scale = 1.0 / math.sqrt(chan)
+    pair = lax.axis_index("pairs")
+    row = lax.axis_index("rows")
+    col = lax.axis_index("cols")
+    twin = 1 - row
+    orders = [1] + [k for k in range(ncols - 1, 1, -1)]
+
+    def peer(dp, dr, dc):
+        return (lax.rem(pair + dp, npairs), lax.rem(row + dr, 2), lax.rem(col + dc, ncols))
+
+    group = [(dp, dr) for dr in range(2) for dp in range(npairs) if (dp, dr) != (0, 0)]
+    barrier = pltpu.get_barrier_semaphore()
+    for dc in range(1, ncols):
+        pl.semaphore_signal(barrier, inc=1, device_id=peer(0, 0, dc), device_id_type=MESH)
+    for dp, dr in group:
+        pl.semaphore_signal(barrier, inc=1, device_id=peer(dp, dr, 0), device_id_type=MESH)
+    pl.semaphore_wait(barrier, ncols - 1 + len(group))
+
+    def place(c, r):
+        return pl.ds(pl.multiple_of(c * chip + r * krows, 64), krows)
+
+    own = place(col, row)
+    sends = []
+
+    def send(src, dst, ssem, rsem, device):
+        copy = pltpu.make_async_remote_copy(
+            src_ref=src, dst_ref=dst, send_sem=ssem, recv_sem=rsem,
+            device_id=device, device_id_type=MESH,
+        )
+        copy.start()
+        sends.append(copy)
+        return copy
+
+    twin_copies = {0: send(x2_ref.at[0], x2all.at[own], s_send.at[0], s_recv.at[0], peer(0, 1, 0))}
+    z_copies = {}
+    for k in orders:
+        z_copies[k] = send(
+            x2_ref.at[0], x2all.at[own], z_send.at[k], z_recv.at[k], peer(0, 0, k)
+        )
+
+    weight = w_ref[...]
+    x2all[own, :] = x2_ref[0]
+    x_one = x1_ref[0]
+    p1 = jnp.dot(x_one, weight, preferred_element_type=jnp.float32).astype(jnp.bfloat16)
+    p1s[...] = p1
+    pick = (
+        lax.broadcasted_iota(jnp.int32, (part, chan), 1)
+        == lax.broadcasted_iota(jnp.int32, (part, chan), 0) + part * col
+    ).astype(jnp.float32)
+    wt = weight.astype(jnp.float32).T
+    proj = jnp.concatenate([wt, pick], axis=0).astype(jnp.bfloat16)
+    x_one_t = last_dims(pick.astype(jnp.bfloat16), x_one).astype(jnp.bfloat16)
+
+    def matched(best, c, r):
+        at = place(c, r)
+        feat = jnp.dot(x2all[at, :], weight, preferred_element_type=jnp.float32)
+        values = last_dims(feat.astype(jnp.bfloat16), p1s[...])
+        score[at, :] = values
+        return jnp.maximum(best, jnp.max(values.reshape(krows // 8, 8, qrows), axis=0))
+
+    def lefts(c):
+        at = pl.ds(pl.multiple_of(c * chip, 128), chip)
+        left[:, at] = last_dims(proj, x2all[at, :]).astype(jnp.bfloat16)
+
+    best = jnp.full((8, qrows), -jnp.inf, jnp.float32)
+    best = matched(best, col, row)
+    twin_copies[0].wait_recv()
+    best = matched(best, col, twin)
+    lefts(col)
+    for k in orders:
+        source = lax.rem(col + ncols - k, ncols)
+        at = place(source, row)
+        z_copies[k].wait_recv()
+        twin_copies[k] = send(
+            x2all.at[at], x2all.at[at], s_send.at[k], s_recv.at[k], peer(0, 1, 0)
+        )
+        best = matched(best, source, row)
+        twin_copies[k].wait_recv()
+        best = matched(best, source, twin)
+        lefts(source)
+    top = jnp.max(best, axis=0, keepdims=True)
+
+    lanes = 256
+    per = krows // 64
+    nblk = keys // 64
+
+    def where(blk):
+        c = blk // (2 * per)
+        r = lax.rem(blk, 2 * per) // per
+        index = (r * ncols + c) * per + lax.rem(blk, per)
+        y = (index // 2).astype(jnp.float32) * coord_unit
+        x = lax.rem(index, 2).astype(jnp.float32) * (64 * coord_unit)
+        return x, y
+
+    sub = lax.broadcasted_iota(jnp.int32, (8, lanes), 0).astype(jnp.float32) * coord_unit
+    for q in range(0, qrows, lanes):
+        cut = slice(q, q + lanes)
+        tile_top = top[:, cut]
+
+        def sums(blk, carry):
+            acc, acc_x, acc_y = carry
+            at = pl.ds(pl.multiple_of(blk * 64, 64), 64)
+            expo = jnp.exp((score[at, cut] - tile_top) * scale)
+            score[at, cut] = expo
+            rows = [expo[8 * g : 8 * g + 8] for g in range(8)]
+            plain = rows[0]
+            tilted = rows[1] * (8 * coord_unit)
+            for g in range(1, 8):
+                plain = plain + rows[g]
+                if g > 1:
+                    tilted = tilted + rows[g] * (8 * g * coord_unit)
+            x, y = where(blk)
+            return acc + plain, acc_x + (tilted + plain * x), acc_y + plain * y
+
+        zero = jnp.zeros((8, lanes), jnp.float32)
+        acc, acc_x, acc_y = lax.fori_loop(0, nblk, sums, (zero, zero, zero), unroll=2)
+        total = jnp.sum(acc, axis=0, keepdims=True)
+        mean_x = jnp.sum(acc_x + acc * sub, axis=0, keepdims=True) / total
+        mean_y = jnp.sum(acc_y, axis=0, keepdims=True) / total
+        index = row * qrows + q + lax.broadcasted_iota(jnp.int32, (1, lanes), 1)
+        flow_ref[0, 0:1, cut] = mean_x - (index % IMG_W).astype(jnp.float32) * coord_unit
+        flow_ref[0, 1:2, cut] = mean_y - (index // IMG_W).astype(jnp.float32) * coord_unit
+        cot_x = cot_ref[0, 0:1, cut]
+        cot_y = cot_ref[0, 1:2, cut]
+        inverse = 1.0 / total
+        offset = cot_x * mean_x + cot_y * mean_y
+        table[:, cut] = (
+            lax.broadcasted_iota(jnp.int32, (64, lanes), 0).astype(jnp.float32) * coord_unit * cot_x
+        )
+
+        def tilt(blk, carry):
+            at = pl.ds(pl.multiple_of(blk * 64, 64), 64)
+            x, y = where(blk)
+            base = cot_x * x + cot_y * y - offset
+            prob = score[at, cut] * inverse
+            slope[at, cut] = (prob * (table[:, cut] + base)).astype(jnp.bfloat16)
+            return carry
+
+        lax.fori_loop(0, nblk, tilt, 0, unroll=2)
+
+    here = pl.ds(pl.multiple_of(col * chip + row * krows, 64), krows)
+    there = pl.ds(pl.multiple_of(col * chip + twin * krows, 64), krows)
+    two_out[...] = jnp.dot(slope[there, :], p1s[...], preferred_element_type=jnp.float32)
+    two_copy = send(two_out, two_in, s_send.at[ncols], s_recv.at[ncols], peer(0, 1, 0))
+    both = jnp.dot(left[...], slope[...], preferred_element_type=jnp.float32)
+    one_t = both[:chan] * scale
+    mixed = both[chan:] * scale
+    term = jnp.zeros((part, chan), jnp.float32)
+    for piece in pieces(mixed):
+        term = term + jnp.dot(piece, p1s[...], preferred_element_type=jnp.float32)
+    for piece in pieces(one_t):
+        term = term + last_dims(x_one_t, piece)
+    slot = pair * 2 + row
+    terms[slot] = term
+    term_copies = []
+    for i, (dp, dr) in enumerate(group):
+        term_copies.append(
+            send(terms.at[slot], terms.at[slot], t_send.at[i], t_recv.at[i], peer(dp, dr, 0))
+        )
+
+    two_mine = jnp.dot(slope[here, :], p1s[...], preferred_element_type=jnp.float32)
+    g1_ref[0] = last_dims(one_t.T.astype(jnp.bfloat16), weight)
+    two_copy.wait_recv()
+    two = (two_mine + two_in[...]) * scale
+    g2_ref[0] = last_dims(two.astype(jnp.bfloat16), weight)
+
+    for copy in term_copies:
+        copy.wait_recv()
+    full = terms[0]
+    for i in range(1, 2 * npairs):
+        full = full + terms[i]
+    blocks[col] = full * (1.0 / math.sqrt(npairs * qrows * 2))
+    block_copies = [
+        send(blocks.at[col], blocks.at[col], b_send.at[k], b_recv.at[k], peer(0, 0, k))
+        for k in range(1, ncols)
+    ]
+    for copy in block_copies:
+        copy.wait_recv()
+    gw_ref[...] = blocks[...].reshape(chan, chan)
+    for copy in sends:
+        copy.wait_send()
+
+
+def one_kernel(npairs, ncols):
+    def call(frame_one, frame_two, weight, flow_cot):
+        qrows, chan = frame_one.shape[1:]
+        krows = frame_two.shape[1]
+        keys = krows * 2 * ncols
+        part = chan // ncols
+        vmem = pl.BlockSpec(memory_space=pltpu.VMEM)
+        dma = pltpu.SemaphoreType.DMA
+        return pl.pallas_call(
+            functools.partial(fused, npairs, ncols),
+            out_shape=(
+                jax.ShapeDtypeStruct(flow_cot.shape, jnp.float32),
+                jax.ShapeDtypeStruct(frame_one.shape, jnp.float32),
+                jax.ShapeDtypeStruct(frame_two.shape, jnp.float32),
+                jax.ShapeDtypeStruct(weight.shape, jnp.float32),
+            ),
+            in_specs=[vmem] * 4,
+            out_specs=(vmem,) * 4,
+            scratch_shapes=[
+                pltpu.VMEM((keys, chan), jnp.bfloat16),
+                pltpu.VMEM((qrows, chan), jnp.bfloat16),
+                pltpu.VMEM((keys, qrows), jnp.float32),
+                pltpu.VMEM((keys, qrows), jnp.bfloat16),
+                pltpu.VMEM((chan + part, keys), jnp.bfloat16),
+                pltpu.VMEM((64, qrows), jnp.float32),
+                pltpu.VMEM((krows, chan), jnp.float32),
+                pltpu.VMEM((krows, chan), jnp.float32),
+                pltpu.VMEM((2 * npairs, part, chan), jnp.float32),
+                pltpu.VMEM((ncols, part, chan), jnp.float32),
+                dma((ncols,)),
+                dma((ncols,)),
+                dma((ncols + 1,)),
+                dma((ncols + 1,)),
+                dma((2 * npairs - 1,)),
+                dma((2 * npairs - 1,)),
+                dma((ncols,)),
+                dma((ncols,)),
+            ],
+            compiler_params=pltpu.CompilerParams(
+                collective_id=0, has_side_effects=True, vmem_limit_bytes=40 * 2**20
+            ),
+        )(frame_one, frame_two, weight, flow_cot)
+
+    return call
+
+
+def fits(mesh, frame_one, frame_two):
+    npairs, nrows, ncols = (mesh.shape[name] for name in ("pairs", "rows", "cols"))
+    pairs, pos, chan = frame_one.shape
+    qrows = pos // nrows
+    krows = pos // (nrows * ncols)
+    return (
+        pairs == npairs
+        and nrows == 2
+        and ncols > 1
+        and chan % (16 * ncols) == 0
+        and qrows % 256 == 0
+        and krows % 64 == 0
+        and IMG_W == 128
+        and pos * qrows * 6 <= 24 * 2**20
+    )
+
+
 def solution(mesh):
     in_specs = (
         P("pairs", "rows", None),
@@ -131,4 +407,13 @@
         P("pairs", ("rows", "cols"), None),
         P(),
     )
-    return jax.shard_map(shards, mesh=mesh, in_specs=in_specs, out_specs=out_specs, check_vma=False)
+
+    def program(frame_one, frame_two, weight, flow_cot):
+        body = shards
+        if fits(mesh, frame_one, frame_two):
+            body = one_kernel(mesh.shape["pairs"], mesh.shape["cols"])
+        return jax.shard_map(
+            body, mesh=mesh, in_specs=in_specs, out_specs=out_specs, check_vma=False
+        )(frame_one, frame_two, weight, flow_cot)
+
+    return program

time: 199 us -> 33.1 us (0.17)
  waiting for transfers between devices: 115 us -> 0 us
  blocking collectives: 53.6 us -> 0 us
  Pallas kernels: 0 us -> 26.3 us
  between operations: 14.2 us -> 0.65 us
  matrix products: 10.2 us -> 0 us
  local copies, waits for them, and re-layouts: 1.68 us -> 5.78 us
  other arithmetic: 2.13 us -> 0 us
    psum x1 -> x0, waiting for transfers between devices: 115 us -> none  [shards(): lax.psum(term, ('pairs', 'rows', 'cols'))]
    psum x2 -> x0, blocking collectives: 38.3 us -> none  [the longest x1 22.8 us: shards(): feat_one_grad = lax.psum(part_one, 'cols')]
    pallas_call x0 -> x1, Pallas kernels: none -> 26.3 us  [call(): pl.pallas_call(functools.partial(fused, npairs, ncols), out_shape=(jax.Sh...]
    pmax x1 -> x0, blocking collectives: 13.3 us -> none  [shards(): peak = lax.pmax(top, 'cols')]
    dot_general x11 -> x0, matrix products: 10.2 us -> none  [the longest x2 2.31 us: lead_product(): lax.dot_general(left, right, (((0,), (0,)), ((), ())), precision=lax.Prec...]
    unnamed x9 -> x12, local copies, waits for them, and re-layouts: 1.62 us -> 5.78 us
  transfers between devices with their start and end apart: 2 -> 0, of which waited for: 1 -> 0; matrix products, arithmetic and copies ran while one was open for 2% -> 0% of each run, Pallas kernels for 0% -> 0%
where the time goes in v1:
time: 33.1 us; the launch traced here: 32.8 us
  Pallas kernels  26.3 us (79%)
  local copies, waits for them, and re-layouts  5.78 us (17%)
  between operations  0.65 us (2%)
    pallas_call x1, Pallas kernels, call(): pl.pallas_call(functools.partial(fused, npairs, ncols), out_shape=(jax.Sh...  26.3 us
    unnamed x12, local copies, waits for them, and re-layouts  5.78 us

profile of v1, /device:TPU:0, one launch (start us, length us, event | category | flops | bytes accessed | tf_op | source)
XLA Modules:
  0.0 32.8 jit_solution(10629806039629310376)
XLA Ops:
  0.6 0.0 copy-start
  0.6 0.9 %copy-done = bf16[1,768,128]{2,1,0:T(8,128)(2,1)S(1)} copy-done((bf16[1,768,128]{2,1,0:T(8,128)(2,1)S(1)}, bf16[1,768,128]{2,1,0:T(8,128)(2,1)}, u32[]{:S(2)}) %copy-start) | copy-done | bytes 196632
  1.6 0.0 copy-start.1
  1.6 0.8 %copy-done.1 = bf16[1,192,128]{2,1,0:T(8,128)(2,1)S(1)} copy-done((bf16[1,192,128]{2,1,0:T(8,128)(2,1)S(1)}, bf16[1,192,128]{2,1,0:T(8,128)(2,1)}, u32[]{:S(2)}) %copy-start.1) | copy-done | bytes 49176
  2.4 0.0 copy-start.2
  2.4 0.8 %copy-done.2 = bf16[128,128]{1,0:T(8,128)(2,1)S(1)} copy-done((bf16[128,128]{1,0:T(8,128)(2,1)S(1)}, bf16[128,128]{1,0:T(8,128)(2,1)}, u32[]{:S(2)}) %copy-start.2) | copy-done | bytes 32792
  3.1 0.0 copy-start.3
  3.1 0.7 %copy-done.3 = f32[1,2,768]{2,1,0:T(2,128)S(1)} copy-done((f32[1,2,768]{2,1,0:T(2,128)S(1)}, f32[1,2,768]{2,1,0:T(2,128)}, u32[]{:S(2)}) %copy-start.3) | copy-done | bytes 6168
  3.8 26.3 %shard_map.75 = (f32[1,2,768]{2,1,0:T(2,128)S(1)}, f32[1,768,128]{2,1,0:T(8,128)S(1)}, f32[1,192,128]{2,1,0:T(8,128)S(1)}, f32[128,128]{1,0:T(8,128)S(1)}) custom-call(bf16[1,768,128]{2,1,0:T(8,128)(2,1)S(1)} %copy-done, bf16[1,192,128]{2,1,0:T(8,128)(2,1)S(1)} %copy-done.1, bf16[128,128]{1,0:T(8,128)(2,1)S(1)} %copy-done.2, f32[1,2,768]{2,1,0:T(2,128)S(1)} %copy-done.3), custom_call_target="tpu_custom_call" | custom-call | tf_op jit(solution)/shard_map/pallas_call | solution.py:342
  30.1 0.6 %copy.12 = f32[1,2,768]{2,1,0:T(2,128)} copy(f32[1,2,768]{2,1,0:T(2,128)S(1)} %get-tuple-element.8) | data formatting | bytes 12288
  30.7 0.7 %copy.13 = f32[1,768,128]{2,1,0:T(8,128)} copy(f32[1,768,128]{2,1,0:T(8,128)S(1)} %get-tuple-element.9) | data formatting | bytes 786432
  31.5 0.6 %copy.14 = f32[1,192,128]{2,1,0:T(8,128)} copy(f32[1,192,128]{2,1,0:T(8,128)S(1)} %get-tuple-element.10) | data formatting | bytes 196608
  32.1 0.6 %copy.15 = f32[128,128]{1,0:T(8,128)} copy(f32[128,128]{1,0:T(8,128)S(1)} %get-tuple-element.11) | data formatting | bytes 131072
Async XLA Ops:
  0.6 0.9 %copy-start = (bf16[1,768,128]{2,1,0:T(8,128)(2,1)S(1)}, bf16[1,768,128]{2,1,0:T(8,128)(2,1)}, u32[]{:S(2)}) copy-start(bf16[1,768,128]{2,1,0:T(8,128)(2,1)} %x1_ref.1) | copy-start | bytes 589828
  1.6 0.8 %copy-start.1 = (bf16[1,192,128]{2,1,0:T(8,128)(2,1)S(1)}, bf16[1,192,128]{2,1,0:T(8,128)(2,1)}, u32[]{:S(2)}) copy-start(bf16[1,192,128]{2,1,0:T(8,128)(2,1)} %x2_ref.1) | copy-start | bytes 147460
  2.4 0.8 %copy-start.2 = (bf16[128,128]{1,0:T(8,128)(2,1)S(1)}, bf16[128,128]{1,0:T(8,128)(2,1)}, u32[]{:S(2)}) copy-start(bf16[128,128]{1,0:T(8,128)(2,1)} %w_ref.1) | copy-start | bytes 98308
  3.1 0.7 %copy-start.3 = (f32[1,2,768]{2,1,0:T(2,128)S(1)}, f32[1,2,768]{2,1,0:T(2,128)}, u32[]{:S(2)}) copy-start(f32[1,2,768]{2,1,0:T(2,128)} %cot_ref.1) | copy-start | bytes 18436

commit v2 on v1

--- a/solution.py
+++ b/solution.py
@@ -138,16 +138,15 @@
 
 def fused(
     npairs, ncols,
-    x1_ref, x2_ref, w_ref, cot_ref,
+    x1_hbm, x2_hbm, w_hbm, cot_hbm,
     flow_ref, g1_ref, g2_ref, gw_ref,
-    x2all, p1s, score, slope, left, table, two_out, two_in, terms, blocks,
-    z_send, z_recv, s_send, s_recv, t_send, t_recv, b_send, b_recv,
+    x1_ref, w_ref, cot_ref, x2all, p1s, score, slope, left, table, two_out, two_in, terms, blocks,
+    z_send, z_recv, s_send, s_recv, t_send, t_recv, b_send, b_recv, load_sem,
 ):
     qrows, chan = x1_ref.shape[1:]
-    krows = x2_ref.shape[1]
+    krows = x2_hbm.shape[1]
     keys = x2all.shape[0]
     chip = 2 * krows
-    part = chan // ncols
     scale = 1.0 / math.sqrt(chan)
     pair = lax.axis_index("pairs")
     row = lax.axis_index("rows")
@@ -158,18 +157,32 @@
     def peer(dp, dr, dc):
         return (lax.rem(pair + dp, npairs), lax.rem(row + dr, 2), lax.rem(col + dc, ncols))
 
-    group = [(dp, dr) for dr in range(2) for dp in range(npairs) if (dp, dr) != (0, 0)]
+    group = [(0, 1)] + [(dp, 0) for dp in range(1, npairs)]
+
+    def place(c, r):
+        return pl.ds(pl.multiple_of(c * chip + r * krows, 64), krows)
+
+    own = place(col, row)
+    loads = [
+        pltpu.make_async_copy(src, dst, load_sem.at[i])
+        for i, (src, dst) in enumerate(
+            [
+                (x2_hbm.at[0], x2all.at[own]),
+                (w_hbm, w_ref),
+                (x1_hbm, x1_ref),
+                (cot_hbm, cot_ref),
+            ]
+        )
+    ]
+    for load in loads:
+        load.start()
     barrier = pltpu.get_barrier_semaphore()
     for dc in range(1, ncols):
         pl.semaphore_signal(barrier, inc=1, device_id=peer(0, 0, dc), device_id_type=MESH)
     for dp, dr in group:
         pl.semaphore_signal(barrier, inc=1, device_id=peer(dp, dr, 0), device_id_type=MESH)
+    loads[0].wait()
     pl.semaphore_wait(barrier, ncols - 1 + len(group))
-
-    def place(c, r):
-        return pl.ds(pl.multiple_of(c * chip + r * krows, 64), krows)
-
-    own = place(col, row)
     sends = []
 
     def send(src, dst, ssem, rsem, device):
@@ -181,21 +194,22 @@
         sends.append(copy)
         return copy
 
-    twin_copies = {0: send(x2_ref.at[0], x2all.at[own], s_send.at[0], s_recv.at[0], peer(0, 1, 0))}
+    twin_copies = {0: send(x2all.at[own], x2all.at[own], s_send.at[0], s_recv.at[0], peer(0, 1, 0))}
     z_copies = {}
     for k in orders:
         z_copies[k] = send(
-            x2_ref.at[0], x2all.at[own], z_send.at[k], z_recv.at[k], peer(0, 0, k)
-        )
-
+            x2all.at[own], x2all.at[own], z_send.at[k], z_recv.at[k], peer(0, 0, k)
+        )
+
+    for load in loads[1:]:
+        load.wait()
     weight = w_ref[...]
-    x2all[own, :] = x2_ref[0]
     x_one = x1_ref[0]
     p1 = jnp.dot(x_one, weight, preferred_element_type=jnp.float32).astype(jnp.bfloat16)
     p1s[...] = p1
     pick = (
-        lax.broadcasted_iota(jnp.int32, (part, chan), 1)
-        == lax.broadcasted_iota(jnp.int32, (part, chan), 0) + part * col
+        lax.broadcasted_iota(jnp.int32, (chan, chan), 1)
+        == lax.broadcasted_iota(jnp.int32, (chan, chan), 0)
     ).astype(jnp.float32)
     wt = weight.astype(jnp.float32).T
     proj = jnp.concatenate([wt, pick], axis=0).astype(jnp.bfloat16)
@@ -225,6 +239,8 @@
             x2all.at[at], x2all.at[at], s_send.at[k], s_recv.at[k], peer(0, 1, 0)
         )
         best = matched(best, source, row)
+    for k in orders:
+        source = lax.rem(col + ncols - k, ncols)
         twin_copies[k].wait_recv()
         best = matched(best, source, twin)
         lefts(source)
@@ -295,40 +311,47 @@
     both = jnp.dot(left[...], slope[...], preferred_element_type=jnp.float32)
     one_t = both[:chan] * scale
     mixed = both[chan:] * scale
-    term = jnp.zeros((part, chan), jnp.float32)
+    term = jnp.zeros((chan, chan), jnp.float32)
     for piece in pieces(mixed):
         term = term + jnp.dot(piece, p1s[...], preferred_element_type=jnp.float32)
     for piece in pieces(one_t):
         term = term + last_dims(x_one_t, piece)
-    slot = pair * 2 + row
-    terms[slot] = term
-    term_copies = []
-    for i, (dp, dr) in enumerate(group):
-        term_copies.append(
-            send(terms.at[slot], terms.at[slot], t_send.at[i], t_recv.at[i], peer(dp, dr, 0))
-        )
-
+    terms[row] = term
+    term_copy = send(terms.at[row], terms.at[row], t_send.at[0], t_recv.at[0], peer(0, 1, 0))
     two_mine = jnp.dot(slope[here, :], p1s[...], preferred_element_type=jnp.float32)
+    term_copy.wait_recv()
+    blocks[pair] = terms[0] + terms[1]
+    block_copies = [
+        send(blocks.at[pair], blocks.at[pair], b_send.at[k], b_recv.at[k], peer(k, 0, 0))
+        for k in range(1, npairs)
+    ]
+
     g1_ref[0] = last_dims(one_t.T.astype(jnp.bfloat16), weight)
     two_copy.wait_recv()
     two = (two_mine + two_in[...]) * scale
     g2_ref[0] = last_dims(two.astype(jnp.bfloat16), weight)
 
-    for copy in term_copies:
-        copy.wait_recv()
-    full = terms[0]
-    for i in range(1, 2 * npairs):
-        full = full + terms[i]
-    blocks[col] = full * (1.0 / math.sqrt(npairs * qrows * 2))
-    block_copies = [
-        send(blocks.at[col], blocks.at[col], b_send.at[k], b_recv.at[k], peer(0, 0, k))
-        for k in range(1, ncols)
-    ]
     for copy in block_copies:
         copy.wait_recv()
-    gw_ref[...] = blocks[...].reshape(chan, chan)
+    full = blocks[0]
+    for i in range(1, npairs):
+        full = full + blocks[i]
+    gw_ref[...] = full * (1.0 / math.sqrt(npairs * qrows * 2))
     for copy in sends:
         copy.wait_send()
+
+
+def store(*refs):
+    half = len(refs) // 2
+    sem = refs[-1]
+    copies = [
+        pltpu.make_async_copy(src, dst, sem.at[i])
+        for i, (src, dst) in enumerate(zip(refs[:half], refs[half:-1]))
+    ]
+    for copy in copies:
+        copy.start()
+    for copy in copies:
+        copy.wait()
 
 
 def one_kernel(npairs, ncols):
@@ -336,43 +359,55 @@
         qrows, chan = frame_one.shape[1:]
         krows = frame_two.shape[1]
         keys = krows * 2 * ncols
-        part = chan // ncols
         vmem = pl.BlockSpec(memory_space=pltpu.VMEM)
         dma = pltpu.SemaphoreType.DMA
-        return pl.pallas_call(
+        hbm = pl.BlockSpec(memory_space=pltpu.HBM)
+        shapes = (
+            jax.ShapeDtypeStruct(flow_cot.shape, jnp.float32),
+            jax.ShapeDtypeStruct(frame_one.shape, jnp.float32),
+            jax.ShapeDtypeStruct(frame_two.shape, jnp.float32),
+            jax.ShapeDtypeStruct(weight.shape, jnp.float32),
+        )
+        outs = pl.pallas_call(
             functools.partial(fused, npairs, ncols),
-            out_shape=(
-                jax.ShapeDtypeStruct(flow_cot.shape, jnp.float32),
-                jax.ShapeDtypeStruct(frame_one.shape, jnp.float32),
-                jax.ShapeDtypeStruct(frame_two.shape, jnp.float32),
-                jax.ShapeDtypeStruct(weight.shape, jnp.float32),
-            ),
-            in_specs=[vmem] * 4,
+            out_shape=tuple(pltpu.VMEM(s.shape, s.dtype) for s in shapes),
+            in_specs=[hbm] * 4,
             out_specs=(vmem,) * 4,
             scratch_shapes=[
+                pltpu.VMEM(frame_one.shape, jnp.bfloat16),
+                pltpu.VMEM(weight.shape, jnp.bfloat16),
+                pltpu.VMEM(flow_cot.shape, jnp.float32),
                 pltpu.VMEM((keys, chan), jnp.bfloat16),
                 pltpu.VMEM((qrows, chan), jnp.bfloat16),
                 pltpu.VMEM((keys, qrows), jnp.float32),
                 pltpu.VMEM((keys, qrows), jnp.bfloat16),
-                pltpu.VMEM((chan + part, keys), jnp.bfloat16),
+                pltpu.VMEM((2 * chan, keys), jnp.bfloat16),
                 pltpu.VMEM((64, qrows), jnp.float32),
                 pltpu.VMEM((krows, chan), jnp.float32),
                 pltpu.VMEM((krows, chan), jnp.float32),
-                pltpu.VMEM((2 * npairs, part, chan), jnp.float32),
-                pltpu.VMEM((ncols, part, chan), jnp.float32),
+                pltpu.VMEM((2, chan, chan), jnp.float32),
+                pltpu.VMEM((npairs, chan, chan), jnp.float32),
                 dma((ncols,)),
                 dma((ncols,)),
                 dma((ncols + 1,)),
                 dma((ncols + 1,)),
-                dma((2 * npairs - 1,)),
-                dma((2 * npairs - 1,)),
-                dma((ncols,)),
-                dma((ncols,)),
+                dma((1,)),
+                dma((1,)),
+                dma((npairs,)),
+                dma((npairs,)),
+                dma((4,)),
             ],
             compiler_params=pltpu.CompilerParams(
-                collective_id=0, has_side_effects=True, vmem_limit_bytes=40 * 2**20
+                collective_id=0, has_side_effects=True, vmem_limit_bytes=60 * 2**20
             ),
         )(frame_one, frame_two, weight, flow_cot)
+        return pl.pallas_call(
+            store,
+            out_shape=shapes,
+            in_specs=[vmem] * 4,
+            out_specs=(hbm,) * 4,
+            scratch_shapes=[dma((4,))],
+        )(*(pltpu.with_memory_space_constraint(out, pltpu.VMEM) for out in outs))
 
     return call
 

time: 33.1 us -> 25.9 us (0.78)
  local copies, waits for them, and re-layouts: 5.78 us -> 0 us
  Pallas kernels: 26.3 us -> 25.1 us
    unnamed x12 -> x0, local copies, waits for them, and re-layouts: 5.78 us -> none
    pallas_call x1 -> x2, Pallas kernels: 26.3 us -> 25.1 us  [the longest x1 24.2 us: call(): pl.pallas_call(functools.partial(fused, npairs, ncols), out_shape=tuple((...]
where the time goes in v2:
time: 25.9 us; the launch traced here: 25.7 us
  Pallas kernels  25.1 us (97%)
  between operations  0.64 us (2%)
    pallas_call x1, Pallas kernels, call(): pl.pallas_call(functools.partial(fused, npairs, ncols), out_shape=tuple((...  24.2 us
    pallas_call x1, Pallas kernels, call(): pl.pallas_call(store, out_shape=shapes, in_specs=[vmem] * 4, out_specs=(h...  0.83 us

profile of v2, /device:TPU:0, one launch (start us, length us, event | category | flops | bytes accessed | tf_op | source)
XLA Modules:
  0.0 25.7 jit_solution(6900226539775004385)
XLA Ops:
  0.6 24.2 %shard_map.75 = (f32[1,2,768]{2,1,0:T(2,128)S(1)}, f32[1,768,128]{2,1,0:T(8,128)S(1)}, f32[1,192,128]{2,1,0:T(8,128)S(1)}, f32[128,128]{1,0:T(8,128)S(1)}) custom-call(bf16[1,768,128]{2,1,0:T(8,128)(2,1)} %x1_hbm.1, bf16[1,192,128]{2,1,0:T(8,128)(2,1)} %x2_hbm.1, bf16[128,128]{1,0:T(8,128)(2,1)} %w_hbm.1, f32[1,2,768]{2,1,0:T(2,128)} %cot_hbm.1), custom_call_target="tpu_custom_call" | custom-call | tf_op jit(solution)/shard_map/pallas_call | solution.py:371
  24.9 0.8 %shard_map.76 = (f32[1,2,768]{2,1,0:T(2,128)}, f32[1,768,128]{2,1,0:T(8,128)}, f32[1,192,128]{2,1,0:T(8,128)}, f32[128,128]{1,0:T(8,128)}) custom-call(f32[1,2,768]{2,1,0:T(2,128)S(1)} %get-tuple-element.8.refs_0_, f32[1,768,128]{2,1,0:T(8,128)S(1)} %get-tuple-element.9.refs_1_, f32[1,192,128]{2,1,0:T(8,128)S(1)} %get-tuple-element.10.refs_2_, ...), custom_call_target="tpu_custom_call" | custom-call | tf_op jit(solution)/shard_map/pallas_call | solution.py:404

commit v3 on v2

--- a/solution.py
+++ b/solution.py
@@ -125,9 +125,7 @@
 def pieces(value):
     high = value.astype(jnp.bfloat16)
     rest = value - high.astype(jnp.float32)
-    mid = rest.astype(jnp.bfloat16)
-    low = (rest - mid.astype(jnp.float32)).astype(jnp.bfloat16)
-    return high, mid, low
+    return jnp.concatenate([high, rest.astype(jnp.bfloat16)], axis=0)
 
 
 def last_dims(left, right):
@@ -140,12 +138,11 @@
     npairs, ncols,
     x1_hbm, x2_hbm, w_hbm, cot_hbm,
     flow_ref, g1_ref, g2_ref, gw_ref,
-    x1_ref, w_ref, cot_ref, x2all, p1s, score, slope, left, table, two_out, two_in, terms, blocks,
+    x1_ref, w_ref, cot_ref, x2all, p1s, score, slope, left, table, stats, two_out, two_in, terms, blocks,
     z_send, z_recv, s_send, s_recv, t_send, t_recv, b_send, b_recv, load_sem,
 ):
     qrows, chan = x1_ref.shape[1:]
     krows = x2_hbm.shape[1]
-    keys = x2all.shape[0]
     chip = 2 * krows
     scale = 1.0 / math.sqrt(chan)
     pair = lax.axis_index("pairs")
@@ -213,109 +210,108 @@
     ).astype(jnp.float32)
     wt = weight.astype(jnp.float32).T
     proj = jnp.concatenate([wt, pick], axis=0).astype(jnp.bfloat16)
-    x_one_t = last_dims(pick.astype(jnp.bfloat16), x_one).astype(jnp.bfloat16)
-
-    def matched(best, c, r):
-        at = place(c, r)
-        feat = jnp.dot(x2all[at, :], weight, preferred_element_type=jnp.float32)
-        values = last_dims(feat.astype(jnp.bfloat16), p1s[...])
-        score[at, :] = values
-        return jnp.maximum(best, jnp.max(values.reshape(krows // 8, 8, qrows), axis=0))
-
-    def lefts(c):
+
+    lanes = 256
+    per = krows // 64
+
+    def where(c, blk):
+        index = (blk // per * ncols + c) * per + blk % per
+        if isinstance(c, int):
+            return index % 2 * (64 * coord_unit), index // 2 * coord_unit
+        y = (index // 2).astype(jnp.float32) * coord_unit
+        x = lax.rem(index, 2).astype(jnp.float32) * (64 * coord_unit)
+        return x, y
+
+    sub = lax.broadcasted_iota(jnp.int32, (8, lanes), 0).astype(jnp.float32) * coord_unit
+
+    def matched(c):
         at = pl.ds(pl.multiple_of(c * chip, 128), chip)
-        left[:, at] = last_dims(proj, x2all[at, :]).astype(jnp.bfloat16)
-
-    best = jnp.full((8, qrows), -jnp.inf, jnp.float32)
-    best = matched(best, col, row)
-    twin_copies[0].wait_recv()
-    best = matched(best, col, twin)
-    lefts(col)
-    for k in orders:
-        source = lax.rem(col + ncols - k, ncols)
-        at = place(source, row)
+        found = x2all[at, :]
+        feat = jnp.dot(found, weight, preferred_element_type=jnp.float32).astype(jnp.bfloat16)
+        for q in range(0, qrows, lanes):
+            cut = slice(q, q + lanes)
+            values = last_dims(feat, p1s[cut, :])
+            best = jnp.max(jnp.max(values.reshape(chip // 8, 8, lanes), axis=0), axis=0, keepdims=True)
+            expo = jnp.exp((values - best) * scale)
+            score[at, cut] = expo
+            acc = acc_x = acc_y = jnp.zeros((8, lanes), jnp.float32)
+            for blk in range(2 * per):
+                rows = [expo[64 * blk + 8 * g : 64 * blk + 8 * g + 8] for g in range(8)]
+                plain = rows[0]
+                tilted = rows[1] * (8 * coord_unit)
+                for g in range(1, 8):
+                    plain = plain + rows[g]
+                    if g > 1:
+                        tilted = tilted + rows[g] * (8 * g * coord_unit)
+                x, y = where(c, blk)
+                acc = acc + plain
+                acc_x = acc_x + (tilted + plain * x)
+                acc_y = acc_y + plain * y
+            stats[c, 0:1, cut] = best
+            stats[c, 1:2, cut] = jnp.sum(acc, axis=0, keepdims=True)
+            stats[c, 2:3, cut] = jnp.sum(acc_x + acc * sub, axis=0, keepdims=True)
+            stats[c, 3:4, cut] = jnp.sum(acc_y, axis=0, keepdims=True)
+        left[:, at] = last_dims(proj, found).astype(jnp.bfloat16)
+
+    def arrive(k):
+        at = place(lax.rem(col + ncols - k, ncols), row)
         z_copies[k].wait_recv()
         twin_copies[k] = send(
             x2all.at[at], x2all.at[at], s_send.at[k], s_recv.at[k], peer(0, 1, 0)
         )
-        best = matched(best, source, row)
-    for k in orders:
-        source = lax.rem(col + ncols - k, ncols)
+
+    twin_copies[0].wait_recv()
+    matched(col)
+    arrive(orders[0])
+    for i, k in enumerate(orders):
+        if i + 1 < len(orders):
+            arrive(orders[i + 1])
         twin_copies[k].wait_recv()
-        best = matched(best, source, twin)
-        lefts(source)
-    top = jnp.max(best, axis=0, keepdims=True)
-
-    lanes = 256
-    per = krows // 64
-    nblk = keys // 64
-
-    def where(blk):
-        c = blk // (2 * per)
-        r = lax.rem(blk, 2 * per) // per
-        index = (r * ncols + c) * per + lax.rem(blk, per)
-        y = (index // 2).astype(jnp.float32) * coord_unit
-        x = lax.rem(index, 2).astype(jnp.float32) * (64 * coord_unit)
-        return x, y
-
-    sub = lax.broadcasted_iota(jnp.int32, (8, lanes), 0).astype(jnp.float32) * coord_unit
-    for q in range(0, qrows, lanes):
-        cut = slice(q, q + lanes)
-        tile_top = top[:, cut]
-
-        def sums(blk, carry):
-            acc, acc_x, acc_y = carry
-            at = pl.ds(pl.multiple_of(blk * 64, 64), 64)
-            expo = jnp.exp((score[at, cut] - tile_top) * scale)
-            score[at, cut] = expo
-            rows = [expo[8 * g : 8 * g + 8] for g in range(8)]
-            plain = rows[0]
-            tilted = rows[1] * (8 * coord_unit)
-            for g in range(1, 8):
-                plain = plain + rows[g]
-                if g > 1:
-                    tilted = tilted + rows[g] * (8 * g * coord_unit)
-            x, y = where(blk)
-            return acc + plain, acc_x + (tilted + plain * x), acc_y + plain * y
-
-        zero = jnp.zeros((8, lanes), jnp.float32)
-        acc, acc_x, acc_y = lax.fori_loop(0, nblk, sums, (zero, zero, zero), unroll=2)
-        total = jnp.sum(acc, axis=0, keepdims=True)
-        mean_x = jnp.sum(acc_x + acc * sub, axis=0, keepdims=True) / total
-        mean_y = jnp.sum(acc_y, axis=0, keepdims=True) / total
-        index = row * qrows + q + lax.broadcasted_iota(jnp.int32, (1, lanes), 1)
-        flow_ref[0, 0:1, cut] = mean_x - (index % IMG_W).astype(jnp.float32) * coord_unit
-        flow_ref[0, 1:2, cut] = mean_y - (index // IMG_W).astype(jnp.float32) * coord_unit
-        cot_x = cot_ref[0, 0:1, cut]
-        cot_y = cot_ref[0, 1:2, cut]
-        inverse = 1.0 / total
-        offset = cot_x * mean_x + cot_y * mean_y
-        table[:, cut] = (
-            lax.broadcasted_iota(jnp.int32, (64, lanes), 0).astype(jnp.float32) * coord_unit * cot_x
-        )
-
-        def tilt(blk, carry):
-            at = pl.ds(pl.multiple_of(blk * 64, 64), 64)
-            x, y = where(blk)
+        matched(lax.rem(col + ncols - k, ncols))
+
+    tops = [stats[c, 0:1, :] for c in range(ncols)]
+    top = functools.reduce(jnp.maximum, tops)
+    shrinks = [jnp.exp((part - top) * scale) for part in tops]
+
+    def gathered(i):
+        whole = stats[0, i : i + 1, :] * shrinks[0]
+        for c in range(1, ncols):
+            whole = whole + stats[c, i : i + 1, :] * shrinks[c]
+        return whole
+
+    total = gathered(1)
+    mean_x = gathered(2) / total
+    mean_y = gathered(3) / total
+    index = row * qrows + lax.broadcasted_iota(jnp.int32, (1, qrows), 1)
+    flow_ref[0, 0:1, :] = mean_x - (index % IMG_W).astype(jnp.float32) * coord_unit
+    flow_ref[0, 1:2, :] = mean_y - (index // IMG_W).astype(jnp.float32) * coord_unit
+    cot_x = cot_ref[0, 0:1, :]
+    cot_y = cot_ref[0, 1:2, :]
+    inverse = 1.0 / total
+    offset = cot_x * mean_x + cot_y * mean_y
+    table[...] = (
+        lax.broadcasted_iota(jnp.int32, (64, qrows), 0).astype(jnp.float32) * coord_unit * cot_x
+    )
+    both = jnp.zeros((2 * chan, qrows), jnp.float32)
+    for c in range(ncols):
+        factor = inverse * shrinks[c]
+        for blk in range(2 * per):
+            at = pl.ds(c * chip + blk * 64, 64)
+            x, y = where(c, blk)
             base = cot_x * x + cot_y * y - offset
-            prob = score[at, cut] * inverse
-            slope[at, cut] = (prob * (table[:, cut] + base)).astype(jnp.bfloat16)
-            return carry
-
-        lax.fori_loop(0, nblk, tilt, 0, unroll=2)
+            slope[at, :] = (score[at, :] * factor * (table[...] + base)).astype(jnp.bfloat16)
+        at = pl.ds(c * chip, chip)
+        both = both + jnp.dot(left[:, at], slope[at, :], preferred_element_type=jnp.float32)
 
     here = pl.ds(pl.multiple_of(col * chip + row * krows, 64), krows)
     there = pl.ds(pl.multiple_of(col * chip + twin * krows, 64), krows)
     two_out[...] = jnp.dot(slope[there, :], p1s[...], preferred_element_type=jnp.float32)
     two_copy = send(two_out, two_in, s_send.at[ncols], s_recv.at[ncols], peer(0, 1, 0))
-    both = jnp.dot(left[...], slope[...], preferred_element_type=jnp.float32)
     one_t = both[:chan] * scale
     mixed = both[chan:] * scale
-    term = jnp.zeros((chan, chan), jnp.float32)
-    for piece in pieces(mixed):
-        term = term + jnp.dot(piece, p1s[...], preferred_element_type=jnp.float32)
-    for piece in pieces(one_t):
-        term = term + last_dims(x_one_t, piece)
+    by_two = jnp.dot(pieces(mixed), p1s[...], preferred_element_type=jnp.float32)
+    by_one = jnp.dot(pieces(one_t), x1_ref[0], preferred_element_type=jnp.float32)
+    term = by_two[:chan] + by_two[chan:] + (by_one[:chan] + by_one[chan:]).T
     terms[row] = term
     term_copy = send(terms.at[row], terms.at[row], t_send.at[0], t_recv.at[0], peer(0, 1, 0))
     two_mine = jnp.dot(slope[here, :], p1s[...], preferred_element_type=jnp.float32)
@@ -383,6 +379,7 @@
                 pltpu.VMEM((keys, qrows), jnp.bfloat16),
                 pltpu.VMEM((2 * chan, keys), jnp.bfloat16),
                 pltpu.VMEM((64, qrows), jnp.float32),
+                pltpu.VMEM((ncols, 8, qrows), jnp.float32),
                 pltpu.VMEM((krows, chan), jnp.float32),
                 pltpu.VMEM((krows, chan), jnp.float32),
                 pltpu.VMEM((2, chan, chan), jnp.float32),
@@ -424,6 +421,7 @@
         and chan % (16 * ncols) == 0
         and qrows % 256 == 0
         and krows % 64 == 0
+        and qrows % IMG_W == 0
         and IMG_W == 128
         and pos * qrows * 6 <= 24 * 2**20
     )

time: 25.9 us -> 23.1 us (0.89)
  Pallas kernels: 25.1 us -> 22.3 us
    pallas_call x1, Pallas kernels: 24.2 us -> 21.5 us  [call(): pl.pallas_call(functools.partial(fused, npairs, ncols), out_shape=tuple((...]
where the time goes in v3:
time: 23.1 us; the launch traced here: 22.9 us
  Pallas kernels  22.3 us (97%)
  between operations  0.64 us (3%)
    pallas_call x1, Pallas kernels, call(): pl.pallas_call(functools.partial(fused, npairs, ncols), out_shape=tuple((...  21.5 us
    pallas_call x1, Pallas kernels, call(): pl.pallas_call(store, out_shape=shapes, in_specs=[vmem] * 4, out_specs=(h...  0.83 us

profile of v3, /device:TPU:0, one launch (start us, length us, event | category | flops | bytes accessed | tf_op | source)
XLA Modules:
  0.0 22.9 jit_solution(4782133126010038099)
XLA Ops:
  0.6 21.5 %shard_map.75 = (f32[1,2,768]{2,1,0:T(2,128)S(1)}, f32[1,768,128]{2,1,0:T(8,128)S(1)}, f32[1,192,128]{2,1,0:T(8,128)S(1)}, f32[128,128]{1,0:T(8,128)S(1)}) custom-call(bf16[1,768,128]{2,1,0:T(8,128)(2,1)} %x1_hbm.1, bf16[1,192,128]{2,1,0:T(8,128)(2,1)} %x2_hbm.1, bf16[128,128]{1,0:T(8,128)(2,1)} %w_hbm.1, f32[1,2,768]{2,1,0:T(2,128)} %cot_hbm.1), custom_call_target="tpu_custom_call" | custom-call | tf_op jit(solution)/shard_map/pallas_call | solution.py:367
  22.1 0.8 %shard_map.76 = (f32[1,2,768]{2,1,0:T(2,128)}, f32[1,768,128]{2,1,0:T(8,128)}, f32[1,192,128]{2,1,0:T(8,128)}, f32[128,128]{1,0:T(8,128)}) custom-call(f32[1,2,768]{2,1,0:T(2,128)S(1)} %get-tuple-element.8.refs_0_, f32[1,768,128]{2,1,0:T(8,128)S(1)} %get-tuple-element.9.refs_1_, f32[1,192,128]{2,1,0:T(8,128)S(1)} %get-tuple-element.10.refs_2_, ...), custom_call_target="tpu_custom_call" | custom-call | tf_op jit(solution)/shard_map/pallas_call | solution.py:401
